TPU v7x, 32 devices: a whole 2x2x4 slice. The times are simulated.
32 devices in a mesh: stn: 2 (over x), tm: 16 (over z, y, core).
Axes of the slice: x: 2, y: 2, z: 4, core: 2. Of those that a mesh axis runs over, the one named last changes fastest.
Arguments:
- voltages: bfloat16 [64, 2, 32, 8192], P('stn', None, None, 'tm'), may hold values from -6 to 6
- phase_codes: int32 [64, 32, 64], replicated, may hold values from 0 to 255
- dispersion: int32 [64], replicated, may hold values from 1 to 4095
Outputs:
- dedispersed: float32 [64, 2, 32, 8192], P('stn', None, None, 'tm')
All inputs are finite; a program needn't handle non-finite values.
Results may differ from a plain program's by a relative error of at most 0.0003.
Values may be sent and summed in bfloat16 or wider, within the bound.
A program may use at most 128 MiB of HBM per device.

v0:
```python
import math

import jax
import jax.numpy as jnp
from jax import lax
from jax.sharding import PartitionSpec as P

chirp_modulus = 4096
phase_levels = 256


def weight_stack(phase_codes, weight_scale):
    angles = phase_codes.astype(jnp.float32) * (2.0 * math.pi / phase_levels)
    w_real = jnp.cos(angles) * weight_scale
    w_imaginary = jnp.sin(angles) * weight_scale
    return jnp.stack([w_real, w_imaginary], axis=1)


def shard_terms(weights, voltages):
    wr_part = weights[:, 0]
    wi_part = weights[:, 1]
    volt_real = voltages[:, 0]
    volt_imaginary = voltages[:, 1]

    def contract(left, right):
        return jnp.einsum(
            "scb,sct->bct",
            left,
            right,
            preferred_element_type=jnp.float32,
            precision=lax.Precision.HIGHEST,
        )

    real_part = contract(wr_part, volt_real) - contract(wi_part, volt_imaginary)
    imaginary = contract(wr_part, volt_imaginary) + contract(wi_part, volt_real)
    return jnp.stack([real_part, imaginary], axis=1)


def angle_pair(row_ids, column_ids, modulus, direction):
    phase_index = row_ids[:, None] * column_ids[None, :] % modulus
    angles = phase_index.astype(jnp.float32) * (direction * 2.0 * math.pi / modulus)
    return (jnp.cos(angles), jnp.sin(angles))


def along_last(real_part, imaginary, tables):
    cos_part, sin_part = tables

    def contract(left, right):
        return jnp.einsum("...n,nk->...k", left, right, precision=lax.Precision.HIGHEST)

    return (
        contract(real_part, cos_part) - contract(imaginary, sin_part),
        contract(real_part, sin_part) + contract(imaginary, cos_part),
    )


def along_second(real_part, imaginary, tables):
    cos_part, sin_part = tables

    def contract(left, right):
        return jnp.einsum("...nl,nk->...kl", left, right, precision=lax.Precision.HIGHEST)

    return (
        contract(real_part, cos_part) - contract(imaginary, sin_part),
        contract(real_part, sin_part) + contract(imaginary, cos_part),
    )


def rotate(real_part, imaginary, tables):
    cos_part, sin_part = tables
    return (
        real_part * cos_part - imaginary * sin_part,
        real_part * sin_part + imaginary * cos_part,
    )


def chirp_pair(dm_values, channel_ids, frequency, length, channel_total):
    centered = jnp.where(frequency < length // 2, frequency, frequency - length)
    squares = centered * centered % chirp_modulus
    chirp_rate = dm_values[:, None] * (2 * channel_total - channel_ids)[None, :] % chirp_modulus
    phase_index = chirp_rate[:, :, None, None] * squares[None, None] % chirp_modulus
    angles = phase_index.astype(jnp.float32) * (-2.0 * math.pi / chirp_modulus)
    return (jnp.cos(angles), jnp.sin(angles))


def body(voltages, phase_codes, dispersion):
    stn_count = lax.axis_size("stn")
    group_size = voltages.shape[0]
    channels = voltages.shape[2]
    local_time = voltages.shape[3]
    beam_total = phase_codes.shape[2]
    station_total = phase_codes.shape[0]
    own_beams = beam_total // stn_count
    own_start = lax.axis_index("stn") * own_beams
    weight_scale = 1.0 / math.sqrt(station_total)
    group_start = lax.axis_index("stn") * group_size
    local_codes = lax.dynamic_slice_in_dim(phase_codes, group_start, group_size, 0)
    weights = weight_stack(local_codes, weight_scale)
    beams = lax.psum_scatter(shard_terms(weights, voltages), "stn", scatter_dimension=0, tiled=True)
    time_shards = lax.axis_size("tm")
    time_rank = lax.axis_index("tm")
    length = time_shards * local_time
    shard_ids = jnp.arange(time_shards, dtype=jnp.int32)
    sample_ids = jnp.arange(local_time, dtype=jnp.int32)
    dm_values = lax.dynamic_slice_in_dim(dispersion, own_start, own_beams)
    inverse_length = 1.0 / length
    column_width = local_time // time_shards
    layout = beams.reshape(own_beams, 2, channels, 1, local_time)
    layout = lax.all_to_all(layout, "tm", split_axis=4, concat_axis=3, tiled=True)
    real_part, imaginary = along_second(
        layout[:, 0], layout[:, 1], angle_pair(shard_ids, shard_ids, time_shards, -1.0)
    )
    global_samples = time_rank * column_width + jnp.arange(column_width, dtype=jnp.int32)
    real_part, imaginary = rotate(
        real_part, imaginary, angle_pair(shard_ids, global_samples, length, -1.0)
    )
    layout = lax.all_to_all(
        jnp.stack([real_part, imaginary], axis=1), "tm", split_axis=3, concat_axis=4, tiled=True
    )
    real_part, imaginary = along_last(
        layout[:, 0], layout[:, 1], angle_pair(sample_ids, sample_ids, local_time, -1.0)
    )
    frequency = time_rank + time_shards * sample_ids[None, :]
    channel_ids = jnp.arange(channels, dtype=jnp.int32)
    real_part, imaginary = rotate(
        real_part, imaginary, chirp_pair(dm_values, channel_ids, frequency, length, channels)
    )
    real_part, imaginary = along_last(
        real_part, imaginary, angle_pair(sample_ids, sample_ids, local_time, 1.0)
    )
    rank_ids = jnp.reshape(time_rank, (1,))
    real_part, imaginary = rotate(
        real_part, imaginary, angle_pair(rank_ids, sample_ids, length, 1.0)
    )
    layout = lax.all_to_all(
        jnp.stack([real_part, imaginary], axis=1), "tm", split_axis=4, concat_axis=3, tiled=True
    )
    real_part, imaginary = along_second(
        layout[:, 0], layout[:, 1], angle_pair(shard_ids, shard_ids, time_shards, 1.0)
    )
    layout = jnp.stack([real_part, imaginary], axis=1) * inverse_length
    layout = lax.all_to_all(layout, "tm", split_axis=3, concat_axis=4, tiled=True)
    return layout.reshape(own_beams, 2, channels, local_time)


def solution(mesh):
    return jax.shard_map(
        body,
        mesh=mesh,
        in_specs=(P("stn", None, None, "tm"), P(), P()),
        out_specs=P("stn", None, None, "tm"),
        check_vma=False,
    )
```

profile of v0, /device:TPU:15, one launch (start us, length us, event | category | flops | bytes accessed | tf_op | source)
XLA Modules:
  0.0 1097.7 jit_solution(11434147133994737201)
XLA Ops:
  6.5 1.8 fusion.196
  8.3 0.1 copy-done
  8.4 4.5 fusion.46
  12.9 4.5 fusion.47
  17.4 4.6 subtract_bitcast_fusion.2
  22.0 4.5 add_bitcast_fusion.2
  26.5 4.3 pad_maximum_fusion.1
  30.8 99.6 %reduce-scatter.2.cloned.1.call-done = f32[32,2,32,512]{3,0,2,1:T(8,128)} async-done(((f32[64,2,32,512]{3,0,2,1:T(8,128)}), f32[32,2,32,512]{3,0,2,1:T(8,128)}) %reduce-scatter.2.cloned.1.call-update) | async-done | bytes 4194320 | tf_op jit(solution)/shard_map/reduce_scatter | solution.py:99
  130.4 14.4 %copy.25 = f32[32,2,32,1,512]{0,2,1,3,4:T(8,128)} copy(f32[32,2,32,1,512]{4,0,2,1,3:T(8,128)} %bitcast.155) | data formatting | bytes 8388608 | tf_op jit(solution)/shard_map/reshape | solution.py:108
  144.8 16.0 %reshape.265 = f32[16,1,65536]{2,1,0:T(1,128)} reshape(f32[512,1,2,32,32]{4,3,2,1,0:T(8,128)} %bitcast.147) | data formatting | bytes 8388608
  160.8 6.7 all-to-all-start
  167.6 0.1 fusion.98
  167.6 92.2 %all-to-all-done = f32[16,1,65536]{2,1,0:T(1,128)} async-done(((f32[16,1,65536]{2,1,0:T(1,128)}), f32[16,1,65536]{2,1,0:T(1,128)}, u32[]{:S(2)}, u32[]{:S(2)}) %all-to-all-start) | async-done | bytes 4194336 | tf_op jit(solution)/shard_map/all_to_all | solution.py:109
  259.9 0.5 broadcast.405
  260.3 13.7 %reduce = f32[16,65536]{1,0:T(8,128)} reduce(f32[16,1,65536]{2,1,0:T(1,128)} %all-to-all-done, f32[]{:T(128)} %broadcast.405), dimensions={1}, to_apply=%all_to_all.14.reduce_sub_computation | reduce | bytes 8388612 | tf_op jit(solution)/shard_map/all_to_all | solution.py:109
  274.0 15.1 %reshape.266 = f32[512,1,2,32,32]{4,3,2,1,0:T(8,128)} reshape(f32[16,65536]{1,0:T(8,128)} %reduce) | data formatting | bytes 8388608
  289.1 10.6 fusion.195
  299.7 11.5 %copy.43 = f32[32,1,32,16,32]{4,3,2,0,1:T(8,128)} copy(f32[32,1,32,16,32]{0,2,1,4,3:T(8,128)} %get-tuple-element.9) | data formatting | bytes 4194304
  311.3 12.4 %fusion.10 = f32[16,32,32,32]{3,0,2,1:T(8,128)} fusion(f32[32,1,32,16,32]{4,3,2,0,1:T(8,128)} %copy.43), kind=kOutput, calls=%fused_computation.13 | convolution fusion | flops 100666880 | bytes 4194304 | tf_op jit(solution)/shard_map/...nl,nk->...kl/dot_general | solution.py:61
  323.6 9.8 fusion.8
  333.4 11.5 %copy.42 = f32[32,1,32,16,32]{4,3,2,0,1:T(8,128)} copy(f32[32,1,32,16,32]{0,2,1,4,3:T(8,128)} %get-tuple-element.10) | data formatting | bytes 4194304
  344.9 11.5 %fusion.12 = f32[16,32,32,32]{3,0,2,1:T(8,128)} fusion(f32[32,1,32,16,32]{4,3,2,0,1:T(8,128)} %copy.42), kind=kOutput, calls=%fused_computation.15 | convolution fusion | flops 100666880 | bytes 4194304 | tf_op jit(solution)/shard_map/...nl,nk->...kl/dot_general | solution.py:61
  356.5 18.7 %subtract_bitcast_fusion.1 = (f32[32,1,32,16,32]{4,3,2,0,1:T(8,128)}, f32[32,1,32,16,32]{4,3,2,0,1:T(8,128)}) fusion(f32[16,32]{1,0:T(8,128)S(1)} %get-tuple-element.16, f32[16,32]{1,0:T(8,128)S(1)} %get-tuple-element.15, f32[16,32,32,32]{3,0,2,1:T(8,128)} %fusion.12, f32[16,32,32,32]{3,0,2,1:T(8,128)} %fusion.8, f32[16,32,32,32]{3,0,2,1:T(8,128)} %fusion.10, ...), kind=kOutput, calls=%fused_computation.22 | convolution fusion | flops 104861184 | bytes 12587008 | tf_op jit(solution)/shard_map/...nl,nk->...kl/dot_general | solution.py:61
  375.1 6.9 pad_maximum_fusion
  382.1 10.6 copy.70
  392.7 16.0 %reshape.267 = f32[16,1,65536]{2,1,0:T(1,128)} reshape(f32[16,2,32,32,32]{4,3,2,1,0:T(8,128)} %bitcast.151) | data formatting | bytes 8388608
  408.7 5.4 all-to-all-start.1
  414.1 0.1 dynamic_slice.7
  414.2 0.1 fusion.120
  414.3 0.1 add_select_fusion.2
  414.4 92.1 %all-to-all-done.1 = f32[16,1,65536]{2,1,0:T(1,128)} async-done(((f32[16,1,65536]{2,1,0:T(1,128)}), f32[16,1,65536]{2,1,0:T(1,128)}, u32[]{:S(2)}, u32[]{:S(2)}) %all-to-all-start.1) | async-done | bytes 4194336 | tf_op jit(solution)/shard_map/all_to_all | solution.py:117
  506.4 13.7 %reduce.1 = f32[16,65536]{1,0:T(8,128)} reduce(f32[16,1,65536]{2,1,0:T(1,128)} %all-to-all-done.1, f32[]{:T(128)} %broadcast.405), dimensions={1}, to_apply=%all_to_all.16.reduce_sub_computation | reduce | bytes 8388612 | tf_op jit(solution)/shard_map/all_to_all | solution.py:117
  520.1 15.1 %reshape.268 = f32[16,2,32,32,32]{4,3,2,1,0:T(8,128)} reshape(f32[16,65536]{1,0:T(8,128)} %reduce.1) | data formatting | bytes 8388608
  535.2 20.4 %copy.28 = f32[32,2,32,16,32]{4,3,2,0,1:T(8,128)} copy(f32[32,2,32,16,32]{4,2,0,1,3:T(8,128)} %bitcast.152) | data formatting | bytes 8388608 | tf_op jit(solution)/shard_map/all_to_all | solution.py:117
  555.6 13.3 %all_to_all.17 = f32[32,2,32,1,512]{4,2,0,3,1:T(8,128)} reshape(f32[32,2,32,16,32]{4,3,2,0,1:T(8,128)} %copy.28) | data formatting | bytes 8388608 | tf_op jit(solution)/shard_map/all_to_all | solution.py:117
  568.9 9.0 fusion.24
  578.0 7.5 fusion.23
  585.5 7.4 fusion.27
  592.9 7.6 fusion.28
  600.5 16.3 %fusion.35 = f32[32,32,512]{2,1,0:T(8,128)S(1)} fusion(f32[32,32,512]{2,1,0:T(8,128)S(1)} %fusion.28, f32[32,32,512]{2,1,0:T(8,128)S(1)} %fusion.27, s32[512]{0:T(512)S(1)} %add_select_fusion.6, s32[32,32]{1,0:T(8,128)S(1)} %add_select_fusion.2), kind=kOutput, calls=%fused_computation.59 | convolution fusion | flops 3233808384 | bytes 6297600 | tf_op jit(solution)/shard_map/...n,nk->...k/dot_general | solution.py:49
  616.8 16.6 %fusion.31 = f32[32,32,512]{2,1,0:T(8,128)S(1)} fusion(f32[32,32,512]{2,1,0:T(8,128)S(1)} %fusion.28, f32[32,32,512]{2,1,0:T(8,128)S(1)} %fusion.27, s32[512]{0:T(512)S(1)} %add_select_fusion.6, s32[32,32]{1,0:T(8,128)S(1)} %add_select_fusion.2), kind=kOutput, calls=%fused_computation.55 | convolution fusion | flops 3233808384 | bytes 6297600 | tf_op jit(solution)/shard_map/...n,nk->...k/dot_general | solution.py:49
  633.4 16.4 %convolution_add_fusion = f32[32,32,512]{2,1,0:T(8,128)S(1)} fusion(f32[32,32,512]{2,1,0:T(8,128)S(1)} %fusion.31, f32[32,32,512]{2,1,0:T(8,128)S(1)} %fusion.28, f32[32,32,512]{2,1,0:T(8,128)S(1)} %fusion.27, s32[512]{0:T(512)S(1)} %add_select_fusion.6, s32[32,32]{1,0:T(8,128)S(1)} %add_select_fusion.2), kind=kOutput, calls=%fused_computation.46 | convolution fusion | flops 3234332672 | bytes 8394752 | tf_op jit(solution)/shard_map/...n,nk->...k/dot_general | solution.py:49
  649.8 16.8 %subtract_bitcast_fusion.3 = (f32[32,1,32,1,512]{4,2,0,3,1:T(8,128)S(1)}, f32[32,1,32,1,512]{4,2,0,3,1:T(8,128)S(1)}) fusion(f32[32,32,512]{2,1,0:T(8,128)S(1)} %convolution_add_fusion, f32[512]{0:T(512)S(1)} %get-tuple-element.17, f32[512]{0:T(512)S(1)} %get-tuple-element.18, f32[32,32,512]{2,1,0:T(8,128)S(1)} %fusion.35, f32[32,32,512]{2,1,0:T(8,128)S(1)} %fusion.28, ...), kind=kOutput, calls=%fused_computation.37 | convolution fusion | flops 3237478400 | bytes 12593152 | tf_op jit(solution)/shard_map/...n,nk->...k/dot_general | solution.py:49
  666.6 2.5 pad_maximum_fusion.2
  669.2 14.4 %copy.29 = f32[32,2,32,1,512]{2,0,3,1,4:T(8,128)} copy(f32[32,2,32,1,512]{4,2,0,3,1:T(8,128)} %pad_maximum_fusion.2) | data formatting | bytes 8388608 | tf_op jit(solution)/shard_map/stack | solution.py:136
  683.5 16.0 %reshape.269 = f32[16,1,65536]{2,1,0:T(1,128)} reshape(f32[512,2,1,32,32]{4,3,2,1,0:T(8,128)} %bitcast.148) | data formatting | bytes 8388608
  699.5 97.7 %all_to_all.45 = f32[16,1,65536]{2,1,0:T(1,128)} all-to-all(f32[16,1,65536]{2,1,0:T(1,128)} %reshape.269), channel_id=1, replica_groups=mesh['stn'=2,'tm'=16] {'tm'}, dimensions={0} | all-to-all | bytes 8388608 | tf_op jit(solution)/shard_map/all_to_all | solution.py:135
  797.2 13.7 %reduce.2 = f32[16,65536]{1,0:T(8,128)} reduce(f32[16,1,65536]{2,1,0:T(1,128)} %all_to_all.45, f32[]{:T(128)} %broadcast.405), dimensions={1}, to_apply=%all_to_all.18.reduce_sub_computation | reduce | bytes 8388612 | tf_op jit(solution)/shard_map/all_to_all | solution.py:135
  810.8 15.1 %reshape.270 = f32[512,2,1,32,32]{4,3,2,1,0:T(8,128)} reshape(f32[16,65536]{1,0:T(8,128)} %reduce.2) | data formatting | bytes 8388608
  826.0 10.6 fusion.194
  836.5 10.1 copy.45
  846.7 12.3 %fusion.2 = f32[16,32,32,32]{3,0,2,1:T(8,128)} fusion(f32[32,1,32,16,32]{4,3,2,0,1:T(8,128)} %copy.45), kind=kOutput, calls=%fused_computation.5 | convolution fusion | flops 100666880 | bytes 4194304 | tf_op jit(solution)/shard_map/...nl,nk->...kl/dot_general | solution.py:61
  859.0 9.6 fusion
  868.6 10.1 copy.44
  878.7 11.0 %subtract_bitcast_fusion = f32[32,1,32,16,32]{4,3,2,0,1:T(8,128)S(1)} fusion(f32[16,32,32,32]{3,0,2,1:T(8,128)} %fusion.2, f32[32,1,32,16,32]{4,3,2,0,1:T(8,128)} %copy.44), kind=kOutput, calls=%fused_computation.20 | convolution fusion | flops 101191168 | bytes 6291456 | tf_op jit(solution)/shard_map/...nl,nk->...kl/dot_general | solution.py:61
  889.8 9.4 add_bitcast_fusion
  899.2 5.2 maximum_multiply_fusion
  904.4 10.6 copy.69
  915.0 16.0 %reshape.271 = f32[16,1,65536]{2,1,0:T(1,128)} reshape(f32[16,2,32,32,32]{4,3,2,1,0:T(8,128)} %bitcast.153) | data formatting | bytes 8388608
  931.0 97.6 %all_to_all.46 = f32[16,1,65536]{2,1,0:T(1,128)} all-to-all(f32[16,1,65536]{2,1,0:T(1,128)} %reshape.271), channel_id=1, replica_groups=mesh['stn'=2,'tm'=16] {'tm'}, dimensions={0} | all-to-all | bytes 8388608 | tf_op jit(solution)/shard_map/all_to_all | solution.py:142
  1028.7 13.7 %reduce.3 = f32[16,65536]{1,0:T(8,128)} reduce(f32[16,1,65536]{2,1,0:T(1,128)} %all_to_all.46, f32[]{:T(128)} %broadcast.405), dimensions={1}, to_apply=%all_to_all.40.reduce_sub_computation | reduce | bytes 8388612 | tf_op jit(solution)/shard_map/all_to_all | solution.py:142
  1042.3 15.1 %reshape.272 = f32[16,2,32,32,32]{4,3,2,1,0:T(8,128)} reshape(f32[16,65536]{1,0:T(8,128)} %reduce.3) | data formatting | bytes 8388608
  1057.4 20.0 %copy.32 = f32[32,2,32,16,32]{4,3,2,1,0:T(8,128)} copy(f32[32,2,32,16,32]{4,2,0,1,3:T(8,128)} %bitcast.154) | data formatting | bytes 8388608 | tf_op jit(solution)/shard_map/all_to_all | solution.py:142
  1077.4 13.0 %reshape.256 = f32[32,2,32,512]{3,2,1,0:T(8,128)} reshape(f32[32,2,32,16,32]{4,3,2,1,0:T(8,128)} %copy.32) | data formatting | bytes 8388608 | tf_op jit(solution)/shard_map/reshape | solution.py:143
  (21 shorter events, 0.1 us)
Async XLA Ops:
  6.5 1.9 copy-start
  6.5 123.9 %reduce-scatter.2.cloned.1.call-start = ((), (), s32[]{:S(2)}) async-start(), calls=%async_computation.5 | async-start | bytes 12582912 | tf_op jit(solution)/shard_map/reduce_scatter | solution.py:99
  160.8 99.0 %all-to-all-start = ((f32[16,1,65536]{2,1,0:T(1,128)}), f32[16,1,65536]{2,1,0:T(1,128)}, u32[]{:S(2)}, u32[]{:S(2)}) async-start(f32[16,1,65536]{2,1,0:T(1,128)} %reshape.265), calls=%async_computation.1 | async-start | bytes 8388608 | tf_op jit(solution)/shard_map/all_to_all | solution.py:109
  311.3 12.4 %copy-start.3 = (f32[32,1,32,16,32]{4,3,2,0,1:T(8,128)S(1)}, f32[32,1,32,16,32]{4,3,2,0,1:T(8,128)}, u32[]{:S(2)}) copy-start(f32[32,1,32,16,32]{4,3,2,0,1:T(8,128)} %copy.43) | copy-start | bytes 6291460
  408.7 5.4 copy-start.7
  408.7 97.7 %all-to-all-start.1 = ((f32[16,1,65536]{2,1,0:T(1,128)}), f32[16,1,65536]{2,1,0:T(1,128)}, u32[]{:S(2)}, u32[]{:S(2)}) async-start(f32[16,1,65536]{2,1,0:T(1,128)} %reshape.267), calls=%async_computation.2 | async-start | bytes 8388608 | tf_op jit(solution)/shard_map/all_to_all | solution.py:117
  568.9 9.1 copy-start.6
  846.7 12.3 %copy-start.4 = (f32[32,1,32,16,32]{4,3,2,0,1:T(8,128)S(1)}, f32[32,1,32,16,32]{4,3,2,0,1:T(8,128)}, u32[]{:S(2)}) copy-start(f32[32,1,32,16,32]{4,3,2,0,1:T(8,128)} %copy.45) | copy-start | bytes 6291460
  878.7 11.0 %copy-start.2 = (f32[32,1,32,16,32]{4,3,2,0,1:T(8,128)S(1)}, f32[32,1,32,16,32]{4,3,2,0,1:T(8,128)}, u32[]{:S(2)}) copy-start(f32[32,1,32,16,32]{4,3,2,0,1:T(8,128)} %copy.44) | copy-start | bytes 6291460
  878.7 11.1 %copy-start.5 = (f32[16,32,32,32]{3,0,2,1:T(8,128)S(1)}, f32[16,32,32,32]{3,0,2,1:T(8,128)}, u32[]{:S(2)}) copy-start(f32[16,32,32,32]{3,0,2,1:T(8,128)} %fusion) | copy-start | bytes 6291460
  1077.4 13.0 %copy-start.1 = (s32[64,32,64]{2,1,0:T(8,128)S(1)}, s32[64,32,64]{2,1,0:T(8,128)}, u32[]{:S(2)}) copy-start(s32[64,32,64]{2,1,0:T(8,128)} %param.4) | copy-start | bytes 1572868
Sparse Core Ops, SparseCore 0:
  31.0 99.4 reduce-scatter.1
where the time goes:
time: 1110 us; the launch traced here: 1100 us
  local copies, waits for them, and re-layouts  308 us (28%)
  waiting for transfers between devices  284 us (26%)
  matrix products  210 us (19%)
  blocking collectives  195 us (18%)
  other arithmetic  73.8 us (7%)
  between operations  14 us (1%)
  starting transfers between devices  12.1 us (1%)
    unnamed x28, local copies, waits for them, and re-layouts  168 us
    reduce_scatter x1, waiting for transfers between devices, body(): lax.psum_scatter(shard_terms(weights, voltages), 'stn', scatter_dimension...  99.6 us
    all_to_all x1, blocking collectives, body(): lax.all_to_all(jnp.stack([real_part, imaginary], axis=1), 'tm', split_axi...  97.7 us
    all_to_all x1, blocking collectives, body(): lax.all_to_all(layout, 'tm', split_axis=3, concat_axis=4, tiled=True)  97.6 us
    dot_general x8, matrix products, contract(): jnp.einsum('...n,nk->...k', left, right, precision=lax.Precision.HIGHEST)  97.6 us
    dot_general x8, matrix products, contract(): jnp.einsum('...nl,nk->...kl', left, right, precision=lax.Precision.HIGHEST)  94.7 us
    all_to_all x1, waiting for transfers between devices, body(): lax.all_to_all(layout, 'tm', split_axis=4, concat_axis=3, tiled=True)  92.2 us
    all_to_all x1, waiting for transfers between devices, body(): lax.all_to_all(jnp.stack([real_part, imaginary], axis=1), 'tm', split_axi...  92.1 us
  transfers between devices with their start and end apart: 3, of which 3 were waited for; matrix products, arithmetic and copies ran while one was open for 0% of the time, Pallas kernels for 0%

commit v1 on v0

--- a/solution.py
+++ b/solution.py
@@ -1,8 +1,13 @@
+import functools
 import math
 
 import jax
 import jax.numpy as jnp
+import ml_dtypes
+import numpy as np
 from jax import lax
+from jax.experimental import pallas as pl
+from jax.experimental.pallas import tpu as pltpu
 from jax.sharding import PartitionSpec as P
 
 chirp_modulus = 4096
@@ -143,11 +148,331 @@
     return layout.reshape(own_beams, 2, channels, local_time)
 
 
+MESH = pl.DeviceIdType.MESH
+base_length = chirp_modulus // 2
+lane_count = 128
+code_limit = 32766.0
+
+
+def split_pair(values):
+    high = values.astype(jnp.bfloat16)
+    return high, (values - high.astype(jnp.float32)).astype(jnp.bfloat16)
+
+
+def host_split(values):
+    high = values.astype(ml_dtypes.bfloat16)
+    low = (values - high.astype(np.float64)).astype(ml_dtypes.bfloat16)
+    return np.stack([high, low])
+
+
+def lane_tables():
+    ids = np.arange(lane_count)
+    angles = 2.0 * np.pi * (np.outer(ids, ids) % lane_count) / lane_count
+    cos_part, sin_part = np.cos(angles), np.sin(angles)
+    forward = np.block([[cos_part, -sin_part], [sin_part, cos_part]])
+    inverse = np.block([[cos_part, sin_part], [-sin_part, cos_part]]) / base_length
+    return host_split(forward), host_split(inverse)
+
+
+def twiddle_table(parts):
+    angles = 2.0 * np.pi * np.outer(np.arange(parts), np.arange(lane_count)) / base_length
+    return np.stack([np.cos(angles), np.sin(angles)]).astype(np.float32)
+
+
+def lane_order(width):
+    strands = width // lane_count
+    order = np.zeros((width, width), np.float32)
+    for sample in range(width):
+        order[sample, (sample % strands) * lane_count + sample // strands] = 1.0
+    return order.astype(ml_dtypes.bfloat16)
+
+
+def times_root(value, step, count, direction):
+    real_part, imaginary = value
+    if step == 0:
+        return value
+    if 4 * step == count:
+        return (-imaginary, real_part) if direction > 0 else (imaginary, -real_part)
+    cosine = math.cos(2.0 * math.pi * step / count)
+    sine = direction * math.sin(2.0 * math.pi * step / count)
+    return (real_part * cosine - imaginary * sine, real_part * sine + imaginary * cosine)
+
+
+def short_transform(values, direction):
+    count = len(values)
+    if count == 1:
+        return values
+    even = short_transform(values[0::2], direction)
+    odd = short_transform(values[1::2], direction)
+    low, high = [], []
+    for step in range(count // 2):
+        turned = times_root(odd[step], step, count, direction)
+        low.append((even[step][0] + turned[0], even[step][1] + turned[1]))
+        high.append((even[step][0] - turned[0], even[step][1] - turned[1]))
+    return low + high
+
+
+def unit_circle(index):
+    quarter = chirp_modulus // 4
+    turns = lax.shift_right_arithmetic(index + quarter // 2, quarter.bit_length() - 1)
+    theta = (index - turns * quarter).astype(jnp.float32) * (2.0 * math.pi / chirp_modulus)
+    square = theta * theta
+    sine = theta * (1.0 + square * (-1 / 6 + square * (1 / 120 + square * (-1 / 5040 + square * (1 / 362880)))))
+    cosine = 1.0 + square * (-1 / 2 + square * (1 / 24 + square * (-1 / 720 + square * (1 / 40320 - square / 3628800))))
+    swap = (turns & 1) == 1
+    first = jnp.where(swap, sine, cosine)
+    second = jnp.where(swap, cosine, sine)
+    first = jnp.where(((turns + 1) & 2) == 2, -first, first)
+    second = jnp.where((turns & 2) == 2, -second, second)
+    return first, second
+
+
+def dot(left, right):
+    return jnp.dot(left, right, preferred_element_type=jnp.float32)
+
+
+def dot_split(left, table_ref):
+    high, low = split_pair(left)
+    return dot(high, table_ref[0]) + dot(low, table_ref[0]) + dot(high, table_ref[1])
+
+
+def filter_kernel(
+    stn_count, parts, volt_ref, weight_ref, rate_ref, order_ref, back_ref, fwd_ref, inv_ref, twiddle_ref,
+    out_ref, scale_ref, grid_ref, mid_ref, chirp_ref,
+):
+    width = volt_ref.shape[2]
+    strands = width // lane_count
+    beams = rate_ref.shape[0]
+    own_beams = beams // stn_count
+    rows = 8
+    chunk = 4
+    weight_high, weight_low = split_pair(weight_ref[...])
+
+    @pl.loop(0, parts)
+    def _(part):
+        pieces = [volt_ref[stn * parts + part] for stn in range(stn_count)]
+        block = jnp.concatenate(pieces, axis=0)
+        block = dot(block, order_ref[...]).astype(jnp.bfloat16)
+        grid_ref[part] = dot(weight_high, block) + dot(weight_low, block)
+
+    def tile(step):
+        group, strand = step // strands, step % strands
+        return (
+            pl.ds(pl.multiple_of(group * rows, rows), rows),
+            pl.ds(pl.multiple_of(beams + group * rows, rows), rows),
+            pl.ds(pl.multiple_of(strand * lane_count, lane_count), lane_count),
+            strand,
+        )
+
+    @pl.loop(0, beams // rows * strands)
+    def _(step):
+        top, bottom, lanes, strand = tile(step)
+        values = [(grid_ref[p, top, lanes], grid_ref[p, bottom, lanes]) for p in range(parts)]
+        for k, (real_part, imaginary) in enumerate(short_transform(values, -1)):
+            cosine, sine = twiddle_ref[0, pl.ds(k, 1)], twiddle_ref[1, pl.ds(k, 1)]
+            mid_ref[strand, k, top, :lane_count] = real_part * cosine + imaginary * sine
+            mid_ref[strand, k, top, lane_count:] = imaginary * cosine - real_part * sine
+
+    rates = rate_ref[...]
+
+    @pl.loop(0, parts)
+    def _(part):
+        column = lax.broadcasted_iota(jnp.int32, (beams, lane_count), 1)
+        frequency = part + parts * column
+        squares = (frequency * frequency) & (chirp_modulus - 1)
+        index = (rates * squares) & (chirp_modulus - 1)
+        cosine, sine = unit_circle(index)
+        chirp_ref[0, part] = cosine
+        chirp_ref[1, part] = sine
+
+    groups = parts // chunk
+
+    @pl.loop(0, strands * groups)
+    def _(step):
+        strand, first = step // groups, (step % groups) * chunk
+        some = pl.ds(first, chunk)
+        spectrum = dot_split(mid_ref[strand, some].reshape(chunk * beams, 2 * lane_count), fwd_ref)
+        real_part, imaginary = spectrum[:, :lane_count], spectrum[:, lane_count:]
+        cosine = chirp_ref[0, some].reshape(chunk * beams, lane_count)
+        sine = chirp_ref[1, some].reshape(chunk * beams, lane_count)
+        turned = jnp.concatenate(
+            [real_part * cosine + imaginary * sine, imaginary * cosine - real_part * sine], axis=1
+        )
+        mid_ref[strand, some] = dot_split(turned, inv_ref).reshape(chunk, beams, 2 * lane_count)
+
+    @pl.loop(0, beams // rows * strands)
+    def _(step):
+        top, bottom, lanes, strand = tile(step)
+        values = []
+        for k in range(parts):
+            cosine, sine = twiddle_ref[0, pl.ds(k, 1)], twiddle_ref[1, pl.ds(k, 1)]
+            real_part = mid_ref[strand, k, top, :lane_count]
+            imaginary = mid_ref[strand, k, top, lane_count:]
+            values.append((real_part * cosine - imaginary * sine, real_part * sine + imaginary * cosine))
+        for p, (real_part, imaginary) in enumerate(short_transform(values, 1)):
+            grid_ref[p, top, lanes] = real_part
+            grid_ref[p, bottom, lanes] = imaginary
+
+    row_ids = lax.broadcasted_iota(jnp.int32, (own_beams, lane_count), 0)
+    lane_ids = lax.broadcasted_iota(jnp.int32, (own_beams, lane_count), 1)
+
+    @pl.loop(0, parts)
+    def _(part):
+        high, low = split_pair(grid_ref[part])
+        series = dot(high, back_ref[...]) + dot(low, back_ref[...])
+        peak = jnp.maximum(jnp.max(jnp.abs(series), axis=1, keepdims=True), 1e-30)
+        codes = jnp.round(series * (code_limit / peak)).astype(jnp.int32)
+        words = (codes[:beams] << 16) | (codes[beams:] & 0xFFFF)
+        for stn in range(stn_count):
+            slot = stn * parts + part
+            first = stn * own_beams
+            out_ref[slot] = words[first : first + own_beams]
+            peaks = jnp.where(row_ids == lane_ids, peak[first : first + own_beams], 0.0)
+            second = beams + first
+            peaks += jnp.where(
+                row_ids + own_beams == lane_ids, peak[second : second + own_beams], 0.0
+            )
+            peaks = jnp.sum(peaks, axis=0, keepdims=True)
+            scale_ref[slot] = jnp.broadcast_to(peaks, scale_ref.shape[1:])
+
+
+def filter_channel(stn_count, parts, volts, weights, rates):
+    devices, _, width = volts.shape
+    beams = rates.shape[0]
+    forward, inverse = lane_tables()
+    order = lane_order(width)
+    vmem = pl.BlockSpec(memory_space=pltpu.VMEM)
+    return pl.pallas_call(
+        functools.partial(filter_kernel, stn_count, parts),
+        out_shape=(
+            jax.ShapeDtypeStruct((devices, beams // stn_count, width), jnp.int32),
+            jax.ShapeDtypeStruct((devices, 8, lane_count), jnp.float32),
+        ),
+        in_specs=[vmem] * 8,
+        out_specs=(vmem, vmem),
+        scratch_shapes=[
+            pltpu.VMEM((parts, 2 * beams, width), jnp.float32),
+            pltpu.VMEM((width // lane_count, parts, beams, 2 * lane_count), jnp.float32),
+            pltpu.VMEM((2, parts, beams, lane_count), jnp.float32),
+        ],
+        compiler_params=pltpu.CompilerParams(vmem_limit_bytes=40 * 2**20),
+        name="filter_channel",
+    )(
+        volts, weights, rates, jnp.asarray(order), jnp.asarray(order.T), jnp.asarray(forward),
+        jnp.asarray(inverse), jnp.asarray(twiddle_table(parts)),
+    )
+
+
+def exchange_kernel(stn_count, parts, count, *refs):
+    ins, outs = refs[:count], refs[count : 2 * count]
+    send_sems, recv_sems, copy_sems = refs[2 * count :]
+    devices = stn_count * parts
+    me = lax.axis_index("stn") * parts + lax.axis_index("tm")
+
+    def place(device):
+        return (device // parts, device % parts)
+
+    def remote(which, offset, target, slot):
+        return pltpu.make_async_remote_copy(
+            src_ref=ins[which].at[target],
+            dst_ref=outs[which].at[slot],
+            send_sem=send_sems.at[which, offset],
+            recv_sem=recv_sems.at[which, offset],
+            device_id=place(target),
+            device_id_type=MESH,
+        )
+
+    barrier = pltpu.get_barrier_semaphore()
+
+    @pl.loop(1, devices)
+    def _(offset):
+        pl.semaphore_signal(
+            barrier, inc=1, device_id=place(lax.rem(me + offset, devices)), device_id_type=MESH
+        )
+
+    pl.semaphore_wait(barrier, devices - 1)
+
+    @pl.loop(1, devices)
+    def _(offset):
+        target = lax.rem(me + offset, devices)
+        for which in range(count):
+            remote(which, offset, target, me).start()
+
+    own = [
+        pltpu.make_async_copy(ins[which].at[me], outs[which].at[me], copy_sems.at[which])
+        for which in range(count)
+    ]
+    for copy in own:
+        copy.start()
+    for copy in own:
+        copy.wait()
+
+    @pl.loop(1, devices)
+    def _(offset):
+        target = lax.rem(me + offset, devices)
+        origin = lax.rem(me + devices - offset, devices)
+        for which in range(count):
+            remote(which, offset, target, me).wait_send()
+            remote(which, offset, target, origin).wait_recv()
+
+
+def exchange(stn_count, parts, arrays, collective_id):
+    devices = stn_count * parts
+    count = len(arrays)
+    place = pl.BlockSpec(memory_space=pl.ANY)
+    return pl.pallas_call(
+        functools.partial(exchange_kernel, stn_count, parts, count),
+        out_shape=tuple(
+            jax.ShapeDtypeStruct(x.shape, x.dtype) for x in arrays
+        ),
+        in_specs=[place] * count,
+        out_specs=(place,) * count,
+        scratch_shapes=[
+            pltpu.SemaphoreType.DMA((count, devices)),
+            pltpu.SemaphoreType.DMA((count, devices)),
+            pltpu.SemaphoreType.DMA((count,)),
+        ],
+        compiler_params=pltpu.CompilerParams(collective_id=collective_id, has_side_effects=True),
+        name="exchange_%d" % collective_id,
+    )(*arrays)
+
+
+def channel_body(voltages, phase_codes, dispersion):
+    stn_count, parts = lax.axis_size("stn"), lax.axis_size("tm")
+    group_size, _, channels, width = voltages.shape
+    station_total, _, beams = phase_codes.shape
+    channel = lax.axis_index("stn") * parts + lax.axis_index("tm")
+    sent = jnp.transpose(voltages, (2, 0, 1, 3)).reshape(channels, 2 * group_size, width)
+    (volts,) = exchange(stn_count, parts, [sent], 0)
+    codes = lax.dynamic_index_in_dim(phase_codes, channel, 1, keepdims=False).T
+    angles = codes.astype(jnp.float32) * (2.0 * math.pi / phase_levels)
+    w_real = jnp.cos(angles) / math.sqrt(station_total)
+    w_imaginary = jnp.sin(angles) / math.sqrt(station_total)
+    weights = jnp.stack(
+        [jnp.stack([w_real, -w_imaginary], axis=-1), jnp.stack([w_imaginary, w_real], axis=-1)]
+    ).reshape(2 * beams, 2 * station_total)
+    rates = (dispersion * (2 * channels - channel) % chirp_modulus)[:, None]
+    words, peaks = filter_channel(stn_count, parts, volts, weights, rates)
+    words, peaks = exchange(stn_count, parts, [words, peaks], 1)
+    own_beams = beams // stn_count
+    codes = jnp.stack([words >> 16, (words << 16) >> 16], axis=1).astype(jnp.float32)
+    steps = peaks[:, 0, : 2 * own_beams].reshape(channels, 2, own_beams, 1) * (1.0 / code_limit)
+    return jnp.transpose(codes * steps, (2, 1, 0, 3))
+
+
 def solution(mesh):
-    return jax.shard_map(
-        body,
-        mesh=mesh,
-        in_specs=(P("stn", None, None, "tm"), P(), P()),
-        out_specs=P("stn", None, None, "tm"),
-        check_vma=False,
-    )
+    stn_count, parts = mesh.shape["stn"], mesh.shape["tm"]
+
+    def run(voltages, phase_codes, dispersion):
+        channels, length = voltages.shape[2:]
+        by_channel = channels == stn_count * parts and parts * lane_count == base_length
+        by_channel = by_channel and length % base_length == 0
+        return jax.shard_map(
+            channel_body if by_channel else body,
+            mesh=mesh,
+            in_specs=(P("stn", None, None, "tm"), P(), P()),
+            out_specs=P("stn", None, None, "tm"),
+            check_vma=False,
+        )(voltages, phase_codes, dispersion)
+
+    return run

time: 1110 us -> 156 us (0.14)
  local copies, waits for them, and re-layouts: 308 us -> 13.1 us
  waiting for transfers between devices: 284 us -> 0 us
  matrix products: 210 us -> 0 us
  blocking collectives: 195 us -> 0 us
  Pallas kernels: 0 us -> 136 us
  other arithmetic: 73.8 us -> 4.64 us
  between operations: 14 us -> 0.17 us
  starting transfers between devices: 12.1 us -> 0 us
    dot_general x20 -> x0, matrix products: 210 us -> none  [the longest x8 97.6 us: contract(): jnp.einsum('...n,nk->...k', left, right, precision=lax.Precision.HIGHEST)]
    all_to_all x2 -> x0, blocking collectives: 195 us -> none  [the longest x1 97.7 us: body(): lax.all_to_all(jnp.stack([real_part, imaginary], axis=1), 'tm', split_axi...]
    all_to_all x2 -> x0, waiting for transfers between devices: 184 us -> none  [the longest x1 92.2 us: body(): lax.all_to_all(layout, 'tm', split_axis=4, concat_axis=3, tiled=True)]
    unnamed x28 -> x18, local copies, waits for them, and re-layouts: 168 us -> 4.06 us
    pallas_call x0 -> x3, Pallas kernels: none -> 136 us  [the longest x2 107 us: exchange(): pl.pallas_call(functools.partial(exchange_kernel, stn_count, parts, count...]
    reduce_scatter x1 -> x0, waiting for transfers between devices: 99.6 us -> none  [body(): lax.psum_scatter(shard_terms(weights, voltages), 'stn', scatter_dimension...]
    all_to_all x4 -> x0, other arithmetic: 54.6 us -> none  [the longest x2 27.3 us: body(): lax.all_to_all(jnp.stack([real_part, imaginary], axis=1), 'tm', split_axi...]
    all_to_all x4 -> x0, local copies, waits for them, and re-layouts: 54.2 us -> none  [the longest x2 33.7 us: body(): lax.all_to_all(jnp.stack([real_part, imaginary], axis=1), 'tm', split_axi...]
  transfers between devices with their start and end apart: 3 -> 0, of which waited for: 3 -> 0; matrix products, arithmetic and copies ran while one was open for 0% -> 0% of each run, Pallas kernels for 0% -> 0%
where the time goes in v1:
time: 156 us; the launch traced here: 154 us
  Pallas kernels  136 us (87%)
  local copies, waits for them, and re-layouts  13.1 us (8%)
  other arithmetic  4.64 us (3%)
    pallas_call x2, Pallas kernels, exchange(): pl.pallas_call(functools.partial(exchange_kernel, stn_count, parts, count...  107 us
    pallas_call x1, Pallas kernels, filter_channel(): pl.pallas_call(functools.partial(filter_kernel, stn_count, parts), out_sh...  28.9 us
    transpose x1, local copies, waits for them, and re-layouts, channel_body(): return jnp.transpose(codes * steps, (2, 1, 0, 3))  4.44 us
    reshape x1, local copies, waits for them, and re-layouts, channel_body(): jnp.transpose(voltages, (2, 0, 1, 3))  4.08 us
    unnamed x18, local copies, waits for them, and re-layouts  4.06 us

profile of v1, /device:TPU:15, one launch (start us, length us, event | category | flops | bytes accessed | tf_op | source)
XLA Modules:
  0.0 153.8 jit_solution(1325198860993200336)
XLA Ops:
  0.0 0.0 copy-start
  0.0 0.8 fusion.4
  0.8 0.5 copy-done
  1.3 0.1 copy.28.rate_ref
  1.4 0.1 fusion.2
  1.5 0.1 fusion.3
  1.7 0.1 copy.26
  1.8 0.1 reshape.21
  1.9 0.1 copy.27.weight_ref
  2.0 4.1 %copy.31.refs_0_ = bf16[32,64,512]{2,1,0:T(8,128)(2,1)} copy(bf16[32,64,512]{2,0,1:T(8,128)(2,1)} %bitcast.35) | data formatting | bytes 4194304 | tf_op jit(solution)/shard_map/reshape | solution.py:445
  6.1 0.0 copy-start.3
  6.1 0.0 copy-start.4
  6.1 0.0 copy-start.5
  6.1 0.0 copy-start.6
  6.1 0.0 copy-start.8
  6.1 51.6 %exchange_0.1.volt_ref = bf16[32,64,512]{2,1,0:T(8,128)(2,1)} custom-call(bf16[32,64,512]{2,1,0:T(8,128)(2,1)} %copy.31.refs_0_), custom_call_target="tpu_custom_call" | custom-call | tf_op jit(solution)/shard_map/exchange_0/pallas_call | solution.py:423
  57.7 0.0 copy-done.3
  57.8 0.0 copy-done.4
  57.8 0.0 copy-done.5
  57.8 0.0 copy-done.6
  57.8 0.0 copy-done.8
  57.8 0.0 copy-start.1
  57.8 1.6 %copy-done.1 = bf16[32,64,512]{2,1,0:T(8,128)(2,1)S(1)} copy-done((bf16[32,64,512]{2,1,0:T(8,128)(2,1)S(1)}, bf16[32,64,512]{2,1,0:T(8,128)(2,1)}, u32[]{:S(2)}) %copy-start.1) | copy-done | bytes 2097176
  59.4 28.9 %filter_channel.1 = (s32[32,32,512]{2,1,0:T(8,128)S(1)}, f32[32,8,128]{2,1,0:T(8,128)S(1)}) custom-call(bf16[32,64,512]{2,1,0:T(8,128)(2,1)S(1)} %copy-done.1, f32[128,128]{1,0:T(8,128)S(1)} %copy.27.weight_ref, s32[64,1]{1,0:T(8,128)S(1)} %copy.28.rate_ref, bf16[512,512]{1,0:T(8,128)(2,1)S(1)} %copy-done.4, bf16[512,512]{1,0:T(8,128)(2,1)S(1)} %copy-done.3, ...), custom_call_target="tpu_custom_call" | custom-call | tf_op jit(solution)/shard_map/filter_channel/pallas_call | solution.py:345
  88.3 0.0 copy-start.2
  88.3 1.3 copy-done.2
  89.7 0.0 copy-start.7
  89.7 0.6 copy-done.7
  90.3 55.3 %exchange_1.1 = (s32[32,32,512]{2,1,0:T(8,128)}, f32[32,8,128]{2,1,0:T(8,128)}) custom-call(s32[32,32,512]{2,1,0:T(8,128)} %copy-done.2, f32[32,8,128]{2,1,0:T(8,128)} %copy-done.7), custom_call_target="tpu_custom_call" | custom-call | tf_op jit(solution)/shard_map/exchange_1/pallas_call | solution.py:423
  145.6 1.0 multiply_reduce_fusion
  146.6 0.1 mul.46
  146.7 2.3 %shift-right-arithmetic_bitcast_fusion.1 = (s32[32,1,32,512]{3,2,0,1:T(8,128)S(1)}, s32[32,1,32,512]{3,2,0,1:T(8,128)S(1)}) fusion(s32[32,32,512]{2,1,0:T(8,128)} %get-tuple-element.11), kind=kLoop, calls=%fused_computation.4 | loop fusion | flops 1572864 | bytes 6291456 | tf_op jit(solution)/shard_map/stack | solution.py:458
  148.9 0.4 fusion.1
  149.3 4.4 %copy.30 = f32[32,2,32,512]{3,2,1,0:T(8,128)} copy(f32[32,2,32,512]{3,0,2,1:T(8,128)S(1)} %fusion.1) | data formatting | bytes 8388608 | tf_op jit(solution)/shard_map/transpose | solution.py:460
  (4 shorter events, 0.1 us)
Async XLA Ops:
  0.0 1.2 copy-start
  6.1 51.6 %copy-start.3 = (bf16[512,512]{1,0:T(8,128)(2,1)S(1)}, bf16[512,512]{1,0:T(8,128)(2,1)}, u32[]{:S(2)}) copy-start(bf16[512,512]{1,0:T(8,128)(2,1)} %constant.53.clone.back_ref) | copy-start | bytes 1572868
  6.1 51.6 %copy-start.4 = (bf16[512,512]{1,0:T(8,128)(2,1)S(1)}, bf16[512,512]{1,0:T(8,128)(2,1)}, u32[]{:S(2)}) copy-start(bf16[512,512]{1,0:T(8,128)(2,1)} %constant.52.clone.order_ref) | copy-start | bytes 1572868
  6.1 51.7 %copy-start.5 = (bf16[2,256,256]{2,1,0:T(8,128)(2,1)S(1)}, bf16[2,256,256]{2,1,0:T(8,128)(2,1)}, u32[]{:S(2)}) copy-start(bf16[2,256,256]{2,1,0:T(8,128)(2,1)} %constant.55.clone.inv_ref) | copy-start | bytes 786436
  6.1 51.7 %copy-start.6 = (bf16[2,256,256]{2,1,0:T(8,128)(2,1)S(1)}, bf16[2,256,256]{2,1,0:T(8,128)(2,1)}, u32[]{:S(2)}) copy-start(bf16[2,256,256]{2,1,0:T(8,128)(2,1)} %constant.54.clone.fwd_ref) | copy-start | bytes 786436
  6.1 51.7 %copy-start.8 = (f32[2,16,128]{2,1,0:T(8,128)S(1)}, f32[2,16,128]{2,1,0:T(8,128)}, u32[]{:S(2)}) copy-start(f32[2,16,128]{2,1,0:T(8,128)} %constant.56.clone.twiddle_ref) | copy-start | bytes 49156
  57.8 1.6 %copy-start.1 = (bf16[32,64,512]{2,1,0:T(8,128)(2,1)S(1)}, bf16[32,64,512]{2,1,0:T(8,128)(2,1)}, u32[]{:S(2)}) copy-start(bf16[32,64,512]{2,1,0:T(8,128)(2,1)} %exchange_0.1.volt_ref) | copy-start | bytes 6291460
  88.3 1.3 copy-start.2
  89.7 0.7 copy-start.7

commit v2 on v0

--- a/solution.py
+++ b/solution.py
@@ -1,8 +1,13 @@
+import functools
 import math
 
 import jax
 import jax.numpy as jnp
+import ml_dtypes
+import numpy as np
 from jax import lax
+from jax.experimental import pallas as pl
+from jax.experimental.pallas import tpu as pltpu
 from jax.sharding import PartitionSpec as P
 
 chirp_modulus = 4096
@@ -143,11 +148,382 @@
     return layout.reshape(own_beams, 2, channels, local_time)
 
 
+MESH = pl.DeviceIdType.MESH
+base_length = chirp_modulus // 2
+lane_count = 128
+code_limit = 32766.0
+halves = 2
+
+
+def split_pair(values):
+    high = values.astype(jnp.bfloat16)
+    return high, (values - high.astype(jnp.float32)).astype(jnp.bfloat16)
+
+
+def host_split(values):
+    high = values.astype(ml_dtypes.bfloat16)
+    low = (values - high.astype(np.float64)).astype(ml_dtypes.bfloat16)
+    return np.stack([high, low])
+
+
+def lane_tables():
+    ids = np.arange(lane_count)
+    angles = 2.0 * np.pi * (np.outer(ids, ids) % lane_count) / lane_count
+    cos_part, sin_part = np.cos(angles), np.sin(angles)
+    forward = np.block([[cos_part, -sin_part], [sin_part, cos_part]])
+    inverse = np.block([[cos_part, sin_part], [-sin_part, cos_part]]) / base_length
+    return host_split(forward), host_split(inverse)
+
+
+def twiddle_table(parts):
+    angles = 2.0 * np.pi * np.outer(np.arange(parts), np.arange(lane_count)) / base_length
+    return np.stack([np.cos(angles), np.sin(angles)]).astype(np.float32)
+
+
+def lane_order(width):
+    strands = width // lane_count
+    order = np.zeros((width, width), np.float32)
+    for sample in range(width):
+        order[sample, (sample % strands) * lane_count + sample // strands] = 1.0
+    return order.astype(ml_dtypes.bfloat16)
+
+
+def times_root(value, step, count, direction):
+    real_part, imaginary = value
+    if step == 0:
+        return value
+    if 4 * step == count:
+        return (-imaginary, real_part) if direction > 0 else (imaginary, -real_part)
+    cosine = math.cos(2.0 * math.pi * step / count)
+    sine = direction * math.sin(2.0 * math.pi * step / count)
+    return (real_part * cosine - imaginary * sine, real_part * sine + imaginary * cosine)
+
+
+def short_transform(values, direction):
+    count = len(values)
+    if count == 1:
+        return values
+    even = short_transform(values[0::2], direction)
+    odd = short_transform(values[1::2], direction)
+    low, high = [], []
+    for step in range(count // 2):
+        turned = times_root(odd[step], step, count, direction)
+        low.append((even[step][0] + turned[0], even[step][1] + turned[1]))
+        high.append((even[step][0] - turned[0], even[step][1] - turned[1]))
+    return low + high
+
+
+def unit_circle(index):
+    quarter = chirp_modulus // 4
+    turns = lax.shift_right_arithmetic(index + quarter // 2, quarter.bit_length() - 1)
+    theta = (index - turns * quarter).astype(jnp.float32) * (2.0 * math.pi / chirp_modulus)
+    square = theta * theta
+    sine = theta * (1.0 + square * (-1 / 6 + square * (1 / 120 + square * (-1 / 5040 + square * (1 / 362880)))))
+    cosine = 1.0 + square * (-1 / 2 + square * (1 / 24 + square * (-1 / 720 + square * (1 / 40320 - square / 3628800))))
+    swap = (turns & 1) == 1
+    first = jnp.where(swap, sine, cosine)
+    second = jnp.where(swap, cosine, sine)
+    first = jnp.where(((turns + 1) & 2) == 2, -first, first)
+    second = jnp.where((turns & 2) == 2, -second, second)
+    return first, second
+
+
+def dot(left, right):
+    return jnp.dot(left, right, preferred_element_type=jnp.float32)
+
+
+def dot_split(left, table_ref):
+    high, low = split_pair(left)
+    return dot(high, table_ref[0]) + dot(low, table_ref[0]) + dot(high, table_ref[1])
+
+
+def filter_kernel(
+    stn_count, parts, sent_ref, weight_ref, rate_ref, order_ref, back_ref, fwd_ref, inv_ref, twiddle_ref,
+    words_ref, peaks_ref, volt_ref, grid_ref, mid_ref, chirp_ref, word_ref, scale_ref,
+    in_send, in_recv, out_send, out_recv, copy_sems,
+):
+    width = volt_ref.shape[2]
+    strands = width // lane_count
+    beams = rate_ref.shape[0]
+    own_beams = beams // stn_count
+    rows = 8
+    chunk = 8
+    part_beams = own_beams // halves
+    half_beams = beams // halves
+    devices = stn_count * parts
+    time_rank = lax.axis_index("tm")
+    me = lax.axis_index("stn") * parts + time_rank
+
+    def place(device):
+        return (device // parts, device % parts)
+
+    def send_in(target, slot):
+        return pltpu.make_async_remote_copy(
+            src_ref=sent_ref.at[target],
+            dst_ref=volt_ref.at[slot],
+            send_sem=in_send.at[target],
+            recv_sem=in_recv.at[slot],
+            device_id=place(target),
+            device_id_type=MESH,
+        )
+
+    def views(half, slot):
+        some = pl.ds(pl.multiple_of(half * part_beams, part_beams), part_beams)
+        return (word_ref.at[slot, some], words_ref.at[slot, some]), (
+            scale_ref.at[half, slot], peaks_ref.at[half, slot])
+
+    def send_out(which, half, target, slot):
+        return pltpu.make_async_remote_copy(
+            src_ref=views(half, target)[which][0],
+            dst_ref=views(half, slot)[which][1],
+            send_sem=out_send.at[which, half, target],
+            recv_sem=out_recv.at[which, half, slot],
+            device_id=place(target),
+            device_id_type=MESH,
+        )
+
+    barrier = pltpu.get_barrier_semaphore()
+
+    @pl.loop(1, devices)
+    def _(offset):
+        pl.semaphore_signal(
+            barrier, inc=1, device_id=place(lax.rem(me + offset, devices)), device_id_type=MESH
+        )
+
+    pl.semaphore_wait(barrier, devices - 1)
+
+    @pl.loop(1, devices)
+    def _(offset):
+        send_in(lax.rem(me + offset, devices), me).start()
+
+    own = pltpu.make_async_copy(sent_ref.at[me], volt_ref.at[me], copy_sems.at[0])
+    own.start()
+
+    def regroup(values):
+        return jnp.concatenate(
+            [
+                values[stn * own_beams + half * part_beams : stn * own_beams + (half + 1) * part_beams]
+                for half in range(halves)
+                for stn in range(stn_count)
+            ],
+            axis=0,
+        )
+
+    weights = weight_ref[...]
+    weights = jnp.concatenate([regroup(weights[:beams]), regroup(weights[beams:])], axis=0)
+    weight_high, weight_low = split_pair(weights)
+    rates = regroup(rate_ref[...])
+
+    @pl.loop(0, parts)
+    def _(part):
+        column = lax.broadcasted_iota(jnp.int32, (beams, lane_count), 1)
+        frequency = part + parts * column
+        squares = (frequency * frequency) & (chirp_modulus - 1)
+        index = (rates * squares) & (chirp_modulus - 1)
+        cosine, sine = unit_circle(index)
+        chirp_ref[0, part] = cosine
+        chirp_ref[1, part] = sine
+
+    own.wait()
+
+    @pl.loop(0, parts)
+    def _(turn):
+        part = lax.rem(time_rank + parts - turn, parts)
+        for stn in range(stn_count):
+            slot = stn * parts + part
+
+            @pl.when(slot != me)
+            def _():
+                send_in(slot, slot).wait_recv()
+
+        pieces = [volt_ref[stn * parts + part] for stn in range(stn_count)]
+        block = dot(jnp.concatenate(pieces, axis=0), order_ref[...]).astype(jnp.bfloat16)
+        grid_ref[part] = dot(weight_high, block) + dot(weight_low, block)
+
+    def tile(half, step):
+        group, strand = step // strands, step % strands
+        first = half * half_beams + group * rows
+        return (
+            pl.ds(pl.multiple_of(first, rows), rows),
+            pl.ds(pl.multiple_of(beams + first, rows), rows),
+            pl.ds(pl.multiple_of(strand * lane_count, lane_count), lane_count),
+            strand,
+        )
+
+    groups = parts // chunk
+    row_ids = lax.broadcasted_iota(jnp.int32, (part_beams, lane_count), 0)
+    lane_ids = lax.broadcasted_iota(jnp.int32, (part_beams, lane_count), 1)
+
+    @pl.loop(0, halves)
+    def _(half):
+        upper = pl.ds(pl.multiple_of(half * half_beams, half_beams), half_beams)
+        lower = pl.ds(pl.multiple_of(beams + half * half_beams, half_beams), half_beams)
+
+        @pl.loop(0, half_beams // rows * strands)
+        def _(step):
+            top, bottom, lanes, strand = tile(half, step)
+            values = [(grid_ref[p, top, lanes], grid_ref[p, bottom, lanes]) for p in range(parts)]
+            for k, (real_part, imaginary) in enumerate(short_transform(values, -1)):
+                cosine, sine = twiddle_ref[0, pl.ds(k, 1)], twiddle_ref[1, pl.ds(k, 1)]
+                mid_ref[strand, k, top, :lane_count] = real_part * cosine + imaginary * sine
+                mid_ref[strand, k, top, lane_count:] = imaginary * cosine - real_part * sine
+
+        @pl.loop(0, strands * groups)
+        def _(step):
+            strand, first = step // groups, (step % groups) * chunk
+            some = pl.ds(first, chunk)
+            spectrum = dot_split(
+                mid_ref[strand, some, upper].reshape(chunk * half_beams, 2 * lane_count), fwd_ref
+            )
+            real_part, imaginary = spectrum[:, :lane_count], spectrum[:, lane_count:]
+            cosine = chirp_ref[0, some, upper].reshape(chunk * half_beams, lane_count)
+            sine = chirp_ref[1, some, upper].reshape(chunk * half_beams, lane_count)
+            turned = jnp.concatenate(
+                [real_part * cosine + imaginary * sine, imaginary * cosine - real_part * sine], axis=1
+            )
+            mid_ref[strand, some, upper] = dot_split(turned, inv_ref).reshape(
+                chunk, half_beams, 2 * lane_count
+            )
+
+        @pl.loop(0, half_beams // rows * strands)
+        def _(step):
+            top, bottom, lanes, strand = tile(half, step)
+            values = []
+            for k in range(parts):
+                cosine, sine = twiddle_ref[0, pl.ds(k, 1)], twiddle_ref[1, pl.ds(k, 1)]
+                real_part = mid_ref[strand, k, top, :lane_count]
+                imaginary = mid_ref[strand, k, top, lane_count:]
+                values.append(
+                    (real_part * cosine - imaginary * sine, real_part * sine + imaginary * cosine)
+                )
+            for p, (real_part, imaginary) in enumerate(short_transform(values, 1)):
+                grid_ref[p, top, lanes] = real_part
+                grid_ref[p, bottom, lanes] = imaginary
+
+        @pl.loop(0, parts)
+        def _(turn):
+            part = lax.rem(time_rank + 1 + turn, parts)
+            block = jnp.concatenate([grid_ref[part, upper], grid_ref[part, lower]], axis=0)
+            high, low = split_pair(block)
+            series = dot(high, back_ref[...]) + dot(low, back_ref[...])
+            peak = jnp.maximum(jnp.max(jnp.abs(series), axis=1, keepdims=True), 1e-30)
+            codes = jnp.round(series * (code_limit / peak)).astype(jnp.int32)
+            words = (codes[:half_beams] << 16) | (codes[half_beams:] & 0xFFFF)
+            for stn in range(stn_count):
+                slot = stn * parts + part
+                first = stn * part_beams
+                second = half_beams + first
+                word_ref[slot, pl.ds(pl.multiple_of(half * part_beams, part_beams), part_beams)] = words[
+                    first : first + part_beams
+                ]
+                peaks = jnp.where(row_ids == lane_ids, peak[first : first + part_beams], 0.0)
+                peaks += jnp.where(
+                    row_ids + part_beams == lane_ids, peak[second : second + part_beams], 0.0
+                )
+                peaks = jnp.sum(peaks, axis=0, keepdims=True)
+                scale_ref[half, slot] = jnp.broadcast_to(peaks, scale_ref.shape[2:])
+
+                @pl.when(slot != me)
+                def _():
+                    for which in range(2):
+                        send_out(which, half, slot, me).start()
+
+    own = []
+    for half in range(halves):
+        for which, (source, target) in enumerate(views(half, me)):
+            own.append(pltpu.make_async_copy(source, target, copy_sems.at[1 + 2 * half + which]))
+    for copy in own:
+        copy.start()
+    for copy in own:
+        copy.wait()
+
+    @pl.loop(1, devices)
+    def _(offset):
+        other = lax.rem(me + offset, devices)
+        send_in(other, me).wait_send()
+        for half in range(halves):
+            for which in range(2):
+                send_out(which, half, other, me).wait_send()
+                send_out(which, half, other, other).wait_recv()
+
+
+def filter_channel(stn_count, parts, sent, weights, rates):
+    devices, inputs, width = sent.shape
+    beams = rates.shape[0]
+    own_beams = beams // stn_count
+    forward, inverse = lane_tables()
+    order = lane_order(width)
+    vmem = pl.BlockSpec(memory_space=pltpu.VMEM)
+    place = pl.BlockSpec(memory_space=pl.ANY)
+    words_shape = (devices, own_beams, width)
+    peaks_shape = (halves, devices, 8, lane_count)
+    return pl.pallas_call(
+        functools.partial(filter_kernel, stn_count, parts),
+        out_shape=(
+            jax.ShapeDtypeStruct(words_shape, jnp.int32),
+            jax.ShapeDtypeStruct(peaks_shape, jnp.float32),
+        ),
+        in_specs=[place] + [vmem] * 7,
+        out_specs=(place, place),
+        scratch_shapes=[
+            pltpu.VMEM((devices, inputs, width), sent.dtype),
+            pltpu.VMEM((parts, 2 * beams, width), jnp.float32),
+            pltpu.VMEM((width // lane_count, parts, beams, 2 * lane_count), jnp.float32),
+            pltpu.VMEM((2, parts, beams, lane_count), jnp.float32),
+            pltpu.VMEM(words_shape, jnp.int32),
+            pltpu.VMEM(peaks_shape, jnp.float32),
+            pltpu.SemaphoreType.DMA((devices,)),
+            pltpu.SemaphoreType.DMA((devices,)),
+            pltpu.SemaphoreType.DMA((2, halves, devices)),
+            pltpu.SemaphoreType.DMA((2, halves, devices)),
+            pltpu.SemaphoreType.DMA((1 + 2 * halves,)),
+        ],
+        compiler_params=pltpu.CompilerParams(
+            vmem_limit_bytes=44 * 2**20, collective_id=0, has_side_effects=True
+        ),
+        name="filter_channel",
+    )(
+        sent, weights, rates, jnp.asarray(order), jnp.asarray(order.T), jnp.asarray(forward),
+        jnp.asarray(inverse), jnp.asarray(twiddle_table(parts)),
+    )
+
+
+def channel_body(voltages, phase_codes, dispersion):
+    stn_count, parts = lax.axis_size("stn"), lax.axis_size("tm")
+    group_size, _, channels, width = voltages.shape
+    station_total, _, beams = phase_codes.shape
+    channel = lax.axis_index("stn") * parts + lax.axis_index("tm")
+    sent = jnp.transpose(voltages, (2, 0, 1, 3)).reshape(channels, 2 * group_size, width)
+    codes = lax.dynamic_index_in_dim(phase_codes, channel, 1, keepdims=False).T
+    angles = codes.astype(jnp.float32) * (2.0 * math.pi / phase_levels)
+    w_real = jnp.cos(angles) / math.sqrt(station_total)
+    w_imaginary = jnp.sin(angles) / math.sqrt(station_total)
+    weights = jnp.stack(
+        [jnp.stack([w_real, -w_imaginary], axis=-1), jnp.stack([w_imaginary, w_real], axis=-1)]
+    ).reshape(2 * beams, 2 * station_total)
+    rates = (dispersion * (2 * channels - channel) % chirp_modulus)[:, None]
+    words, peaks = filter_channel(stn_count, parts, sent, weights, rates)
+    own_beams = beams // stn_count
+    codes = jnp.stack([words >> 16, (words << 16) >> 16], axis=1).astype(jnp.float32)
+    peaks = peaks[:, :, 0, : 2 * own_beams // halves].reshape(halves, channels, 2, own_beams // halves)
+    peaks = jnp.transpose(peaks, (1, 2, 0, 3)).reshape(channels, 2, own_beams, 1)
+    steps = peaks * (1.0 / code_limit)
+    return jnp.transpose(codes * steps, (2, 1, 0, 3))
+
+
 def solution(mesh):
-    return jax.shard_map(
-        body,
-        mesh=mesh,
-        in_specs=(P("stn", None, None, "tm"), P(), P()),
-        out_specs=P("stn", None, None, "tm"),
-        check_vma=False,
-    )
+    stn_count, parts = mesh.shape["stn"], mesh.shape["tm"]
+
+    def run(voltages, phase_codes, dispersion):
+        channels, length = voltages.shape[2:]
+        by_channel = channels == stn_count * parts and parts * lane_count == base_length
+        by_channel = by_channel and length % base_length == 0
+        return jax.shard_map(
+            channel_body if by_channel else body,
+            mesh=mesh,
+            in_specs=(P("stn", None, None, "tm"), P(), P()),
+            out_specs=P("stn", None, None, "tm"),
+            check_vma=False,
+        )(voltages, phase_codes, dispersion)
+
+    return run

time: 1110 us -> 127 us (0.11); the launches traced: 1100 us -> 127 us
  local copies, waits for them, and re-layouts: 308 us -> 8.44 us
  waiting for transfers between devices: 284 us -> 0 us
  matrix products: 210 us -> 0 us
  blocking collectives: 195 us -> 0 us
  Pallas kernels: 0 us -> 117 us
  other arithmetic: 73.8 us -> 2.03 us
  between operations: 14 us -> 0.17 us
  starting transfers between devices: 12.1 us -> 0 us
    dot_general x20 -> x0, matrix products: 210 us -> none  [the longest x8 97.6 us: contract(): jnp.einsum('...n,nk->...k', left, right, precision=lax.Precision.HIGHEST)]
    all_to_all x2 -> x0, blocking collectives: 195 us -> none  [the longest x1 97.7 us: body(): lax.all_to_all(jnp.stack([real_part, imaginary], axis=1), 'tm', split_axi...]
    all_to_all x2 -> x0, waiting for transfers between devices: 184 us -> none  [the longest x1 92.2 us: body(): lax.all_to_all(layout, 'tm', split_axis=4, concat_axis=3, tiled=True)]
    unnamed x28 -> x12, local copies, waits for them, and re-layouts: 168 us -> 0.52 us
    pallas_call x0 -> x1, Pallas kernels: none -> 117 us  [filter_channel(): pl.pallas_call(functools.partial(filter_kernel, stn_count, parts), out_sh...]
    reduce_scatter x1 -> x0, waiting for transfers between devices: 99.6 us -> none  [body(): lax.psum_scatter(shard_terms(weights, voltages), 'stn', scatter_dimension...]
    all_to_all x4 -> x0, other arithmetic: 54.6 us -> none  [the longest x2 27.3 us: body(): lax.all_to_all(jnp.stack([real_part, imaginary], axis=1), 'tm', split_axi...]
    all_to_all x4 -> x0, local copies, waits for them, and re-layouts: 54.2 us -> none  [the longest x2 33.7 us: body(): lax.all_to_all(jnp.stack([real_part, imaginary], axis=1), 'tm', split_axi...]
  transfers between devices with their start and end apart: 3 -> 0, of which waited for: 3 -> 0; matrix products, arithmetic and copies ran while one was open for 0% -> 0% of each run, Pallas kernels for 0% -> 0%
where the time goes in v2:
time: 127 us
  Pallas kernels  117 us (92%)
  local copies, waits for them, and re-layouts  8.44 us (7%)
  other arithmetic  2.03 us (2%)
    pallas_call x1, Pallas kernels, filter_channel(): pl.pallas_call(functools.partial(filter_kernel, stn_count, parts), out_sh...  117 us
    transpose x1, local copies, waits for them, and re-layouts, channel_body(): return jnp.transpose(codes * steps, (2, 1, 0, 3))  4.44 us
    reshape x1, local copies, waits for them, and re-layouts, channel_body(): jnp.transpose(voltages, (2, 0, 1, 3))  2.86 us

profile of v2, /device:TPU:15, one launch (start us, length us, event | category | flops | bytes accessed | tf_op | source)
XLA Modules:
  0.0 127.3 jit_solution(16511708665701458365)
XLA Ops:
  0.0 0.0 copy-start
  0.0 0.8 fusion.4
  0.8 0.5 copy-done
  1.3 0.1 copy.29.rate_ref
  1.4 0.1 fusion.2
  1.5 0.1 fusion.3
  1.7 0.1 copy.27
  1.8 0.1 reshape.24
  1.9 0.1 copy.28.weight_ref
  2.0 0.0 copy-start.1
  2.1 0.0 copy-start.2
  2.1 0.0 copy-start.3
  2.1 0.0 copy-start.4
  2.1 0.0 copy-start.5
  2.1 2.9 %copy.35.sent_ref = bf16[32,64,512]{2,1,0:T(8,128)(2,1)S(1)} copy(bf16[32,64,512]{2,0,1:T(8,128)(2,1)} %bitcast.40) | data formatting | bytes 4194304 | tf_op jit(solution)/shard_map/reshape | solution.py:496
  5.0 0.0 copy-done.1
  5.0 0.0 copy-done.2
  5.0 0.0 copy-done.3
  5.0 0.0 copy-done.4
  5.0 0.0 copy-done.5
  5.0 116.7 %filter_channel.1 = (s32[32,32,512]{2,1,0:T(8,128)S(1)}, f32[2,32,8,128]{3,2,1,0:T(8,128)S(1)}) custom-call(bf16[32,64,512]{2,1,0:T(8,128)(2,1)S(1)} %copy.35.sent_ref, f32[128,128]{1,0:T(8,128)S(1)} %copy.28.weight_ref, s32[64,1]{1,0:T(8,128)S(1)} %copy.29.rate_ref, bf16[512,512]{1,0:T(8,128)(2,1)S(1)} %copy-done.2, bf16[512,512]{1,0:T(8,128)(2,1)S(1)} %copy-done.1, ...), custom_call_target="tpu_custom_call" | custom-call | tf_op jit(solution)/shard_map/filter_channel/pallas_call | solution.py:460
  121.8 0.1 copy.31
  121.8 0.1 copy.33
  121.9 0.6 shift-right-arithmetic_bitcast_fusion.1
  122.5 0.4 fusion.1
  122.9 4.4 %copy.34 = f32[32,2,32,512]{3,2,1,0:T(8,128)} copy(f32[32,2,32,512]{3,0,2,1:T(8,128)S(1)} %fusion.1) | data formatting | bytes 8388608 | tf_op jit(solution)/shard_map/transpose | solution.py:511
  (6 shorter events, 0.1 us)
Async XLA Ops:
  0.0 1.2 copy-start
  2.0 2.9 %copy-start.1 = (bf16[512,512]{1,0:T(8,128)(2,1)S(1)}, bf16[512,512]{1,0:T(8,128)(2,1)}, u32[]{:S(2)}) copy-start(bf16[512,512]{1,0:T(8,128)(2,1)} %constant.53.clone.back_ref) | copy-start | bytes 1572868
  2.1 2.9 %copy-start.2 = (bf16[512,512]{1,0:T(8,128)(2,1)S(1)}, bf16[512,512]{1,0:T(8,128)(2,1)}, u32[]{:S(2)}) copy-start(bf16[512,512]{1,0:T(8,128)(2,1)} %constant.52.clone.order_ref) | copy-start | bytes 1572868
  2.1 2.9 %copy-start.3 = (bf16[2,256,256]{2,1,0:T(8,128)(2,1)S(1)}, bf16[2,256,256]{2,1,0:T(8,128)(2,1)}, u32[]{:S(2)}) copy-start(bf16[2,256,256]{2,1,0:T(8,128)(2,1)} %constant.55.clone.inv_ref) | copy-start | bytes 786436
  2.1 2.9 %copy-start.4 = (bf16[2,256,256]{2,1,0:T(8,128)(2,1)S(1)}, bf16[2,256,256]{2,1,0:T(8,128)(2,1)}, u32[]{:S(2)}) copy-start(bf16[2,256,256]{2,1,0:T(8,128)(2,1)} %constant.54.clone.fwd_ref) | copy-start | bytes 786436
  2.1 2.9 %copy-start.5 = (f32[2,16,128]{2,1,0:T(8,128)S(1)}, f32[2,16,128]{2,1,0:T(8,128)}, u32[]{:S(2)}) copy-start(f32[2,16,128]{2,1,0:T(8,128)} %constant.56.clone.twiddle_ref) | copy-start | bytes 49156

commit v3 on v2

--- a/solution.py
+++ b/solution.py
@@ -247,7 +247,7 @@
     beams = rate_ref.shape[0]
     own_beams = beams // stn_count
     rows = 8
-    chunk = 8
+    chunk = min(parts, 2 * lane_count * halves // rate_ref.shape[0])
     part_beams = own_beams // halves
     half_beams = beams // halves
     devices = stn_count * parts
@@ -421,7 +421,7 @@
                     row_ids + part_beams == lane_ids, peak[second : second + part_beams], 0.0
                 )
                 peaks = jnp.sum(peaks, axis=0, keepdims=True)
-                scale_ref[half, slot] = jnp.broadcast_to(peaks, scale_ref.shape[2:])
+                scale_ref[half, slot] = peaks
 
                 @pl.when(slot != me)
                 def _():
@@ -456,7 +456,7 @@
     vmem = pl.BlockSpec(memory_space=pltpu.VMEM)
     place = pl.BlockSpec(memory_space=pl.ANY)
     words_shape = (devices, own_beams, width)
-    peaks_shape = (halves, devices, 8, lane_count)
+    peaks_shape = (halves, devices, 1, lane_count)
     return pl.pallas_call(
         functools.partial(filter_kernel, stn_count, parts),
         out_shape=(

time: 127 us -> 122 us (0.961)
  Pallas kernels: 117 us -> 112 us
    pallas_call x1, Pallas kernels: 117 us -> 112 us  [filter_channel(): pl.pallas_call(functools.partial(filter_kernel, stn_count, parts), out_sh...]
where the time goes in v3:
time: 122 us
  Pallas kernels  112 us (92%)
  local copies, waits for them, and re-layouts  8.44 us (7%)
  other arithmetic  2.03 us (2%)
    pallas_call x1, Pallas kernels, filter_channel(): pl.pallas_call(functools.partial(filter_kernel, stn_count, parts), out_sh...  112 us
    transpose x1, local copies, waits for them, and re-layouts, channel_body(): return jnp.transpose(codes * steps, (2, 1, 0, 3))  4.44 us
    reshape x1, local copies, waits for them, and re-layouts, channel_body(): jnp.transpose(voltages, (2, 0, 1, 3))  2.86 us

profile of v3, /device:TPU:15, one launch (start us, length us, event | category | flops | bytes accessed | tf_op | source)
XLA Modules:
  0.0 122.3 jit_solution(3461281767233192573)
XLA Ops:
  0.0 0.0 copy-start
  0.0 0.8 fusion.4
  0.8 0.5 copy-done
  1.3 0.1 copy.29.rate_ref
  1.4 0.1 fusion.2
  1.5 0.1 fusion.3
  1.7 0.1 copy.27
  1.8 0.1 reshape.24
  1.9 0.1 copy.28.weight_ref
  2.0 0.0 copy-start.1
  2.1 0.0 copy-start.2
  2.1 0.0 copy-start.3
  2.1 0.0 copy-start.4
  2.1 0.0 copy-start.5
  2.1 2.9 %copy.35.sent_ref = bf16[32,64,512]{2,1,0:T(8,128)(2,1)S(1)} copy(bf16[32,64,512]{2,0,1:T(8,128)(2,1)} %bitcast.40) | data formatting | bytes 4194304 | tf_op jit(solution)/shard_map/reshape | solution.py:496
  5.0 0.0 copy-done.1
  5.0 0.0 copy-done.2
  5.0 0.0 copy-done.3
  5.0 0.0 copy-done.4
  5.0 0.0 copy-done.5
  5.0 111.6 %filter_channel.1 = (s32[32,32,512]{2,1,0:T(8,128)S(1)}, f32[2,32,1,128]{3,2,1,0:T(1,128)S(1)}) custom-call(bf16[32,64,512]{2,1,0:T(8,128)(2,1)S(1)} %copy.35.sent_ref, f32[128,128]{1,0:T(8,128)S(1)} %copy.28.weight_ref, s32[64,1]{1,0:T(8,128)S(1)} %copy.29.rate_ref, bf16[512,512]{1,0:T(8,128)(2,1)S(1)} %copy-done.2, bf16[512,512]{1,0:T(8,128)(2,1)S(1)} %copy-done.1, ...), custom_call_target="tpu_custom_call" | custom-call | tf_op jit(solution)/shard_map/filter_channel/pallas_call | solution.py:460
  116.7 0.1 copy.31
  116.8 0.1 copy.33
  116.9 0.6 shift-right-arithmetic_bitcast_fusion.1
  117.5 0.4 fusion.1
  117.8 4.4 %copy.34 = f32[32,2,32,512]{3,2,1,0:T(8,128)} copy(f32[32,2,32,512]{3,0,2,1:T(8,128)S(1)} %fusion.1) | data formatting | bytes 8388608 | tf_op jit(solution)/shard_map/transpose | solution.py:511
  (6 shorter events, 0.1 us)
Async XLA Ops:
  0.0 1.2 %copy-start = (s32[64,32,64]{2,1,0:T(8,128)S(1)}, s32[64,32,64]{2,1,0:T(8,128)}, u32[]{:S(2)}) copy-start(s32[64,32,64]{2,1,0:T(8,128)} %param.9) | copy-start | bytes 1572868
  2.0 2.9 %copy-start.1 = (bf16[512,512]{1,0:T(8,128)(2,1)S(1)}, bf16[512,512]{1,0:T(8,128)(2,1)}, u32[]{:S(2)}) copy-start(bf16[512,512]{1,0:T(8,128)(2,1)} %constant.53.clone.back_ref) | copy-start | bytes 1572868
  2.1 2.9 %copy-start.2 = (bf16[512,512]{1,0:T(8,128)(2,1)S(1)}, bf16[512,512]{1,0:T(8,128)(2,1)}, u32[]{:S(2)}) copy-start(bf16[512,512]{1,0:T(8,128)(2,1)} %constant.52.clone.order_ref) | copy-start | bytes 1572868
  2.1 2.9 %copy-start.3 = (bf16[2,256,256]{2,1,0:T(8,128)(2,1)S(1)}, bf16[2,256,256]{2,1,0:T(8,128)(2,1)}, u32[]{:S(2)}) copy-start(bf16[2,256,256]{2,1,0:T(8,128)(2,1)} %constant.55.clone.inv_ref) | copy-start | bytes 786436
  2.1 2.9 %copy-start.4 = (bf16[2,256,256]{2,1,0:T(8,128)(2,1)S(1)}, bf16[2,256,256]{2,1,0:T(8,128)(2,1)}, u32[]{:S(2)}) copy-start(bf16[2,256,256]{2,1,0:T(8,128)(2,1)} %constant.54.clone.fwd_ref) | copy-start | bytes 786436
  2.1 2.9 %copy-start.5 = (f32[2,16,128]{2,1,0:T(8,128)S(1)}, f32[2,16,128]{2,1,0:T(8,128)}, u32[]{:S(2)}) copy-start(f32[2,16,128]{2,1,0:T(8,128)} %constant.56.clone.twiddle_ref) | copy-start | bytes 49156
